TPU v7x, 256 devices: a whole 4x4x8 slice. The times are simulated.
256 devices in a mesh: ctx: 16 (over x, z_hi), head: 8 (over y, core), grp: 2 (over z_lo).
Axes of the slice: x: 4, y: 4, z: 8 (z_hi: 4, z_lo: 2; z = z_hi * 2 + z_lo), core: 2. Of those that a mesh axis runs over, the one named last changes fastest.
Arguments:
- queries: bfloat16 [2, 2048, 8192], P('grp', 'ctx', 'head'), may hold values from -9 to 9
- history_cache: bfloat16 [4, 4096, 8, 256], P(None, 'ctx', 'head'), may hold values from -6 to 6
- fresh_cache: bfloat16 [2, 1024, 8, 256], P('grp', 'ctx', 'head'), may hold values from -6 to 6
- hist_len: int32 [4], replicated, may hold values from 2 to 4096, as said below
- decode_episode: int32 [512], replicated, may hold values from 0 to 3, as said below
Outputs:
- attention: bfloat16 [2, 2048, 8192], P('grp', 'ctx', 'head')
Inputs may be any that keep to these rules, and one draw needn't show every extreme that they name: `hist_len`: one episode's length is exactly 4096 in every draw. `decode_episode`: non-decreasing along the decode rows, with the first row in episode 0 and the last in episode 4 - 1.
All inputs are finite; a program needn't handle non-finite values.
Results may differ from a plain program's by a relative error of at most 0.018.
Values may be sent and summed in bfloat16 or wider, within the bound.
A program may use at most 128 MiB of HBM per device.

v0:
```python
import math

import jax
import jax.numpy as jnp
from jax import lax
from jax.sharding import PartitionSpec as P

STRETCH_TOKENS = 1024
STEPS = 4


masked_score = -1e30


def from_partner(value, axis, stride):
    return lax.ppermute(value, axis, [(i, i ^ 1 << stride) for i in range(lax.axis_size(axis))])


def lookup_small(indices, table):
    hits = indices[:, None] == jnp.arange(table.shape[0], dtype=jnp.int32)[None, :]
    return jnp.sum(jnp.where(hits, table[None, :], 0), axis=1)


def key_layout(shard, hist_len, episode_count, hist_local, new_local, ctx_count):
    hist_rows = episode_count * hist_local
    slot_ids = jnp.arange(hist_rows + 2 * new_local, dtype=jnp.int32)
    is_hist = slot_ids < hist_rows
    within = slot_ids - hist_rows
    key_episode = jnp.where(is_hist, slot_ids // hist_local, 0)
    new_index = within // new_local * new_local * ctx_count + shard * new_local + within % new_local
    key_place = jnp.where(is_hist, shard * hist_local + slot_ids % hist_local, new_index)
    episode_len = lookup_small(key_episode, hist_len)
    return (key_episode, key_place, is_hist, episode_len)


def allowed_mask(layout, query_episode, query_limit):
    key_episode, key_place, is_hist, episode_len = layout
    same_episode = query_episode[:, None] == key_episode[None, :]
    inside = jnp.where(
        is_hist[None, :],
        (key_place < episode_len)[None, :],
        key_place[None, :] <= query_limit[:, None],
    )
    return same_episode & inside


def row_tables(row_ids, group_index, decode_episode):
    decode_rows = lookup_small(row_ids // STEPS, decode_episode)
    query_episode = jnp.where(group_index == 0, 0, decode_rows)
    query_limit = jnp.where(group_index == 0, row_ids, 2 * STRETCH_TOKENS)
    return (query_episode, query_limit)


def block_scores(heads_of_query, key_block, head_dim):
    key_part = key_block[..., :head_dim]
    return jnp.einsum(
        "qhgd,khd->qhgk", heads_of_query, key_part, preferred_element_type=jnp.float32
    ) / math.sqrt(head_dim)


def update_state(state_now, key_block, allowed, heads_of_query, head_dim):
    top_old, total_old, summed_old = state_now
    value_part = key_block[..., head_dim:]
    scores = block_scores(heads_of_query, key_block, head_dim)
    gate = allowed[:, None, None, :]
    top_new = jnp.maximum(top_old, jnp.max(jnp.where(gate, scores, masked_score), axis=-1))
    weights = jnp.where(gate, jnp.exp(scores - top_new[..., None]), 0.0)
    rescale = jnp.exp(top_old - top_new)
    total_new = total_old * rescale + jnp.sum(weights, axis=-1)
    summed_new = summed_old * rescale[..., None] + jnp.einsum(
        "qhgk,khd->qhgd",
        weights.astype(jnp.bfloat16),
        value_part,
        preferred_element_type=jnp.float32,
    )
    return (top_new, total_new, summed_new)


def local(queries, history_cache, fresh_cache, hist_len, decode_episode):
    group_index = lax.axis_index("grp")
    ctx_index = lax.axis_index("ctx")
    ctx_count = lax.axis_size("ctx")
    episode_count, hist_local, kv_local, width = history_cache.shape
    head_dim = width // 2
    own_stretch = fresh_cache[0]
    other_stretch = from_partner(own_stretch, "grp", 0)
    first_stretch = jnp.where(group_index == 0, own_stretch, other_stretch)
    second_stretch = jnp.where(group_index == 0, other_stretch, own_stretch)
    new_local = own_stretch.shape[0]
    slot_pool = jnp.concatenate(
        [
            history_cache.reshape(episode_count * hist_local, kv_local, width),
            first_stretch,
            second_stretch,
        ],
        axis=0,
    )
    pool_rows = slot_pool.shape[0]
    row_count = queries.shape[1]
    query_group = queries.shape[2] // (kv_local * head_dim)
    heads_of_query = queries[0].reshape(row_count, kv_local, query_group, head_dim)
    row_ids = ctx_index * row_count + jnp.arange(row_count, dtype=jnp.int32)
    query_episode, query_limit = row_tables(row_ids, group_index, decode_episode)
    initial = (
        jnp.full((row_count, kv_local, query_group), masked_score, jnp.float32),
        jnp.zeros((row_count, kv_local, query_group), jnp.float32),
        jnp.zeros((row_count, kv_local, query_group, head_dim), jnp.float32),
    )
    slot_piece = lax.all_gather(slot_pool, "ctx", axis=0, tiled=True)
    piece_count = slot_piece.shape[0] // pool_rows
    piece_blocks = slot_piece.reshape(piece_count, pool_rows, kv_local, width)
    shard_ids = jnp.arange(piece_count, dtype=jnp.int32)

    def one_shard(state_inner, shard_item):
        key_block, shard_id = shard_item
        layout = key_layout(shard_id, hist_len, episode_count, hist_local, new_local, ctx_count)
        allowed = allowed_mask(layout, query_episode, query_limit)
        return (update_state(state_inner, key_block, allowed, heads_of_query, head_dim), None)

    state_after, unused_out = lax.scan(one_shard, initial, (piece_blocks, shard_ids))
    top_final, total_final, summed_final = state_after
    result = summed_final / total_final[..., None]
    return result.astype(jnp.bfloat16).reshape(1, row_count, kv_local * query_group * head_dim)


def solution(mesh):
    placed = (
        P("grp", "ctx", "head"),
        P(None, "ctx", "head", None),
        P("grp", "ctx", "head", None),
        P(),
        P(),
    )
    return jax.shard_map(
        local, mesh=mesh, in_specs=placed, out_specs=P("grp", "ctx", "head"), check_vma=False
    )
```

profile of v0, /device:TPU:48, one launch (start us, length us, event | category | flops | bytes accessed | tf_op | source)
XLA Modules:
  0.0 278.4 jit_solution(1212291631325149226)
XLA Ops:
  6.6 4.0 %collective-permute-done = bf16[64,1,256]{2,0,1:T(8,128)(2,1)S(1)} collective-permute-done((bf16[64,1,256]{2,0,1:T(8,128)(2,1)}, bf16[64,1,256]{2,0,1:T(8,128)(2,1)S(1)}, u32[]{:S(2)}, u32[]{:S(2)}) %collective-permute-start) | collective-permute-done | bytes 32800 | tf_op jit(solution)/shard_map/ppermute | solution.py:16
  11.4 1.9 pad_maximum_fusion
  13.4 1.1 copy.16
  15.6 127.8 %all-gather.2.cloned.1.call-done = bf16[18432,1,256]{2,0,1:T(8,128)(2,1)} async-done(((bf16[1152,1,256]{2,0,1:T(8,128)(2,1)}), bf16[18432,1,256]{2,0,1:T(8,128)(2,1)}) %all-gather.2.cloned.1.call-update) | async-done | bytes 9437200 | tf_op jit(solution)/shard_map/all_gather | solution.py:109
  143.3 127.3 %while.18 = (s32[]{:T(128)}, f32[128,1,8]{0,2,1:T(8,128)S(1)}, f32[128,1,8]{0,2,1:T(8,128)S(1)}, f32[128,1,8,128]{0,3,2,1:T(8,128)S(1)}, s32[128]{0:T(128)S(1)},...) while((s32[]{:T(128)}, f32[128,1,8]{0,2,1:T(8,128)S(1)}, ...), condition=%wide.region_5.6_spmd.clone, body=%wide.region_1.5_spmd.clone.sunk | while | flops 615685120 | bytes 17929964 | solution.py:120
  146.2 1.2 select_and_fusion.2
  147.4 1.1 dynamic-slice_bitcast_fusion.2
  154.1 1.2 select_and_fusion.2
  155.4 1.1 dynamic-slice_bitcast_fusion.2
  162.1 1.2 select_and_fusion.2
  170.1 1.2 select_and_fusion.2
  171.3 1.1 dynamic-slice_bitcast_fusion.2
  178.0 1.2 select_and_fusion.2
  179.3 1.1 dynamic-slice_bitcast_fusion.2
  186.0 1.2 select_and_fusion.2
  187.2 1.1 dynamic-slice_bitcast_fusion.2
  193.9 1.2 select_and_fusion.2
  201.9 1.2 select_and_fusion.2
  203.1 1.1 dynamic-slice_bitcast_fusion.2
  209.8 1.2 select_and_fusion.2
  211.1 1.1 dynamic-slice_bitcast_fusion.2
  217.8 1.2 select_and_fusion.2
  225.8 1.2 select_and_fusion.2
  233.7 1.2 select_and_fusion.2
  235.0 1.1 dynamic-slice_bitcast_fusion.2
  241.7 1.2 select_and_fusion.2
  242.9 1.1 dynamic-slice_bitcast_fusion.2
  249.6 1.2 select_and_fusion.2
  257.6 1.2 select_and_fusion.2
  258.8 1.1 dynamic-slice_bitcast_fusion.2
  265.5 1.2 select_and_fusion.2
  266.8 1.1 dynamic-slice_bitcast_fusion.2
  (211 shorter events, 74.8 us)
Async XLA Ops:
  6.5 136.8 %all-gather.2.cloned.1.call-start = ((), (), s32[]{:S(2)}) async-start(), calls=%async_computation | async-start | bytes 10027008 | tf_op jit(solution)/shard_map/all_gather | solution.py:109
  6.5 4.1 %collective-permute-start = (bf16[64,1,256]{2,0,1:T(8,128)(2,1)}, bf16[64,1,256]{2,0,1:T(8,128)(2,1)S(1)}, u32[]{:S(2)}, u32[]{:S(2)}) collective-permute-start(bf16[64,1,256]{2,0,1:T(8,128)(2,1)} %bitcast.106), channel_id=1, source_target_pairs={{0,1},{1,0},{2,3},{3,2},{4,5},{5,4},{6,7},{7,6},{8,9},{9,8},{10,11... | collective-permute-start | bytes 98312 | tf_op jit(solution)/shard_map/ppermute | solution.py:16
Sparse Core Ops, SparseCore 0:
  13.5 129.8 all-gather.1
where the time goes:
time: 280 us; the launch traced here: 278 us
  waiting for transfers between devices  132 us (47%)
  other arithmetic  49.5 us (18%)
  local copies, waits for them, and re-layouts  30.5 us (11%)
  matrix products  29.8 us (11%)
  loops' own time  23.2 us (8%)
  between operations  13.5 us (5%)
    all_gather x1, waiting for transfers between devices, local(): slot_piece = lax.all_gather(slot_pool, 'ctx', axis=0, tiled=True)  128 us
    another operation x1, loops' own time, local(): lax.scan(one_shard, initial, (piece_blocks, shard_ids))  23.2 us
    and x16, other arithmetic, allowed_mask(): return same_episode & inside  20 us
    squeeze x16, local copies, waits for them, and re-layouts, local(): lax.scan(one_shard, initial, (piece_blocks, shard_ids))  17.8 us
    dot_general x16, matrix products, update_state(): jnp.einsum('qhgk,khd->qhgd', weights.astype(jnp.bfloat16), value_part, pr...  16.6 us
    dot_general x16, matrix products, block_scores(): jnp.einsum('qhgd,khd->qhgk', heads_of_query, key_part, preferred_element_...  13.2 us
    reduce_sum x16, other arithmetic, update_state(): total_new = total_old * rescale + jnp.sum(weights, axis=-1)  13 us
    reduce_sum x17, other arithmetic, lookup_small(): return jnp.sum(jnp.where(hits, table[None, :], 0), axis=1)  12.8 us
  transfers between devices with their start and end apart: 2, of which 2 were waited for; matrix products, arithmetic and copies ran while one was open for 1% of the time, Pallas kernels for 0%

commit v1 on v0

v1 whole, which is shorter than its diff:
```python
import functools
import math

import jax
import jax.numpy as jnp
from jax import lax
from jax.experimental import pallas as pl
from jax.experimental.pallas import tpu as pltpu
from jax.sharding import PartitionSpec as P

MESH = pl.DeviceIdType.MESH
STEPS = 4
RING = 4
EPISODES = 4
HEADS = 8
DIM = 128
SLOTS = 256
HALF = 128
NEW = 64
TILE = 32
LANES = TILE * HEADS
ROWS = 128
TILES = ROWS // TILE
MAIN = RING * TILES
EXTRA = EPISODES - 1
STRETCH = 1024
MASKED = -1e30
SCALE = math.log2(math.e) / math.sqrt(DIM)

FROM_RIGHT, FROM_LEFT, FAR_LOW, FAR_HIGH, PAIR, QUERY, RESULT = 0, 9, 18, 23, 28, 29, 35
RELAY = 47
COPIES = 54


def kernel(
    q_ref, hist_ref, fresh_ref, len_in, episode_in, out_ref,
    len_ref, episode_ref, hist_own, hist_d, hist_y, hist_o, fresh_all, q_all,
    acc_o, acc_s, tx_o, tx_s, mid_o, mid_s, fin_o, fin_s, extra_tile,
    send, recv, inside,
):
    ctx = lax.axis_index("ctx")
    grp = lax.axis_index("grp")
    core = lax.axis_index("head") % 2
    x, k = ctx // RING, ctx % RING
    buffers = (hist_own, hist_d, hist_y, hist_o)

    def place(x_at, k_at):
        return (x_at + RING) % RING * RING + (k_at + RING) % RING

    direct = {"ctx": place(x, k + 2 * grp - 1), "grp": 1 - grp}
    partner = {"ctx": ctx, "grp": 1 - grp}
    x_right, x_left = {"ctx": place(x + 1, k)}, {"ctx": place(x - 1, k)}
    z_right, z_left = {"ctx": place(x, k + 1)}, {"ctx": place(x, k - 1)}

    def remote(number, src, dst, device, sender=None):
        return pltpu.make_async_remote_copy(
            src_ref=src, dst_ref=dst, send_sem=send.at[number if sender is None else sender], recv_sem=recv.at[number],
            device_id=device, device_id_type=MESH,
        )

    local_copies = [
        pltpu.make_async_copy(src, dst, inside.at[n])
        for n, (src, dst) in enumerate([
            (len_in, len_ref), (episode_in, episode_ref), (fresh_ref, fresh_all.at[0, grp]),
            (q_ref, q_all.at[pl.ds(0, TILES)]), (hist_ref, hist_own),
        ])
    ]
    for copy in local_copies:
        copy.start()

    barrier = pltpu.get_barrier_semaphore()

    def greet(device):
        pl.semaphore_signal(barrier, inc=1, device_id=device, device_id_type=MESH)

    greet(partner)
    greet(x_right)
    greet(x_left)

    @pl.when(core == 0)
    def _():
        greet(direct)

    @pl.when(core + grp > 0)
    def _():
        greet(z_right)
        greet(z_left)

    pl.semaphore_wait(barrier, jnp.where(core == 1, 5, 4 + 2 * grp))
    for copy in local_copies:
        copy.wait()

    lane = lax.broadcasted_iota(jnp.int32, (1, LANES), 1)
    lane_position = lane % TILE
    slot_row = lax.broadcasted_iota(jnp.int32, (SLOTS, LANES), 0)
    new_row = lax.broadcasted_iota(jnp.int32, (NEW, LANES), 0)

    def half(ref, episode, which):
        if not isinstance(which, int):
            which = pl.multiple_of(which * HALF, HALF)
        else:
            which = which * HALF
        return ref.at[episode, pl.ds(which, HALF)]

    def stack_heads(block):
        return jnp.concatenate([block[:, h * DIM:(h + 1) * DIM] for h in range(HEADS)], axis=0)

    def scores(keys, block):
        return lax.dot_general(keys, stack_heads(block), (((1,), (1,)), ((), ())), preferred_element_type=jnp.float32)

    def update(items, all_scores, all_values, first):
        tops = []
        for parts in all_scores:
            top = jnp.max(parts[0], axis=0, keepdims=True)
            for s in parts[1:]:
                top = jnp.maximum(top, jnp.max(s, axis=0, keepdims=True))
            tops.append(top)
        if not first:
            olds = [(acc_s[i, 0:1], acc_s[i, 1:2]) for i in items]
            tops = [jnp.maximum(top, old[0]) for top, old in zip(tops, olds)]
        weights = [[jnp.exp2(s * SCALE - top * SCALE) for s in parts] for parts, top in zip(all_scores, tops)]
        totals = [sum(jnp.sum(p, axis=0, keepdims=True) for p in parts) for parts in weights]
        sums = [
            sum(
                lax.dot_general(v, p.astype(jnp.bfloat16), (((0,), (0,)), ((), ())), preferred_element_type=jnp.float32)
                for v, p in zip(values, parts)
            )
            for values, parts in zip(all_values, weights)
        ]
        if not first:
            rescales = [jnp.exp2((old[0] - top) * SCALE) for old, top in zip(olds, tops)]
            totals = [total + old[1] * r for total, old, r in zip(totals, olds, rescales)]
            sums = [summed + acc_o[i] * r for i, summed, r in zip(items, sums, rescales)]
        for i, top, total, summed in zip(items, tops, totals, sums):
            acc_s[i, 0:1] = top
            acc_s[i, 1:2] = total
            acc_o[i] = summed

    def merge(one, two):
        top = jnp.maximum(one[0], two[0])
        a, b = jnp.exp2((one[0] - top) * SCALE), jnp.exp2((two[0] - top) * SCALE)
        return top, one[1] * a + two[1] * b, one[2] * a + two[2] * b

    def load(o_ref, s_ref, tile):
        return s_ref[2 * tile:2 * tile + 1], s_ref[2 * tile + 1:2 * tile + 2], o_ref[tile].astype(jnp.float32)

    def span(first, last):
        return list(range(first, last))

    class Copy:
        def __init__(self, number, ends, receives, sender=None):
            self.number, self.ends, self.receives, self.sender = number, ends, receives, sender

        def each(self, wanted, act):
            if all(wanted) and self.ends[0] is self.ends[1]:
                act(0)
                return
            for c in range(2):
                if wanted[c]:
                    pl.when(core == c)(functools.partial(act, c))

        def of(self, ends):
            return remote(self.number, *ends, self.sender)

        def start(self):
            self.each([e is not None for e in self.ends], lambda c: self.of(self.ends[c]).start())

        def wait_send(self):
            self.each([e is not None for e in self.ends], lambda c: self.of(self.ends[c]).wait_send())

        def wait_recv(self):
            ends = self.ends[0] or self.ends[1]
            if all(self.receives):
                self.of(ends).wait_recv()
            else:
                self.each(self.receives, lambda c: self.of(ends).wait_recv())

    def program(prefill):
        me = 0 if prefill else 1
        def either(one, two):
            return {"ctx": jnp.where(core == 1, one["ctx"], two["ctx"])}

        if prefill:
            kv_right, kv_left, q_right, q_left = z_right, z_left, x_right, x_left
            blocks = [place(x, k + off) for off in (0, 1, -1, 2)]
        else:
            kv_right, kv_left = either(x_right, z_right), either(x_left, z_left)
            q_right, q_left = either(z_right, x_right), either(z_left, x_left)
            blocks = [jnp.where(core == 1, place(x + off, k), place(x, k + off)) for off in (0, 1, -1, 2)]

        def row_block(slot):
            off = (0, -1, 1, 2)[slot]
            if prefill:
                return place(x + off, k)
            return jnp.where(core == 1, place(x, k + off), place(x + off, k))

        from_right, from_left, far_low, far_high, relays = {}, {}, {}, {}, {}
        for e in list(range(EPISODES)) + ["new"]:
            ring = not prefill or e in (0, "new")
            n = 2 * EPISODES if e == "new" else 2 * e
            f = EPISODES if e == "new" else e
            for h in range(2 if e != "new" else 1):
                if e == "new":
                    here, right, left = fresh_all.at[0], fresh_all.at[1], fresh_all.at[2]
                    low, to_low = fresh_all.at[1, 0], fresh_all.at[3, 0]
                    high, to_high = fresh_all.at[2, 1], fresh_all.at[3, 1]
                else:
                    here, right, left = half(hist_ref, e, h), half(hist_d, e, h), half(hist_y, e, h)
                    low, to_low = half(hist_d, e, 0), half(hist_o, e, 0)
                    high, to_high = half(hist_y, e, 1), half(hist_o, e, 1)
                key = e if e == "new" else (e, h)
                to_left = (here, right, kv_left)
                to_right = (here, left, kv_right)
                if prefill:
                    from_right[key] = Copy(FROM_RIGHT + n + h, [(here, right, direct), to_left if ring else None], (ring, ring))
                    from_left[key] = Copy(FROM_LEFT + n + h, [None, to_right if ring else None], (ring, ring))
                else:
                    from_right[key] = Copy(FROM_RIGHT + n + h, [None, to_left], (True, True))
                    from_left[key] = Copy(FROM_LEFT + n + h, [to_right, to_right], (True, True))
                    if e in (0, "new"):
                        t = h if e == 0 else 2
                        relays["right", key] = Copy(
                            FROM_RIGHT + n + h, [(right, right, partner), None], (False, False))
                        relays["left", key] = Copy(
                            FROM_LEFT + n + h, [(left, left, partner), None], (False, False), RELAY + t)
            ends = (low, to_low, kv_left)
            ends_high = (high, to_high, kv_right)
            if prefill:
                far_low[e] = Copy(FAR_LOW + f, [None, ends if ring else None], (ring, ring))
                far_high[e] = Copy(FAR_HIGH + f, [None, ends_high if ring else None], (ring, ring))
            else:
                far_low[e] = Copy(FAR_LOW + f, [ends, ends], (True, True))
                far_high[e] = Copy(FAR_HIGH + f, [ends_high, ends_high], (True, True))
                if e in (0, "new"):
                    t = RELAY + 3 + (2 if e == "new" else 0)
                    relays["low", e] = Copy(FAR_LOW + f, [(to_low, to_low, partner), None], (False, False), t)
                    relays["high", e] = Copy(FAR_HIGH + f, [(to_high, to_high, partner), None], (False, False), t + 1)
        late = [] if prefill else [1, 2, 3]
        pair = remote(PAIR, fresh_ref, fresh_all.at[0, me], partner)

        def tiles(slot, part):
            return q_all.at[pl.ds(slot * TILES + part * 2, 2)]

        own_query = [q_ref.at[pl.ds(0, 2)], q_ref.at[pl.ds(2, 2)]]
        queries = [
            remote(QUERY, own_query[0], tiles(1, 0), q_right),
            remote(QUERY + 1, own_query[1], tiles(2, 1), q_left),
            remote(QUERY + 2, own_query[1], tiles(1, 1), q_right),
            remote(QUERY + 3, own_query[0], tiles(2, 0), q_left),
            remote(QUERY + 4, tiles(1, 0), tiles(3, 0), q_right),
            remote(QUERY + 5, tiles(2, 1), tiles(3, 1), q_left),
        ]

        def hand_on(received, onward):
            received.wait_recv()
            onward.start()

        def decode_row(slot, tile):
            return row_block(slot) * (ROWS // STEPS) + tile * (TILE // STEPS)

        def tile_episode(slot, tile):
            return 0 if prefill else episode_ref[decode_row(slot, tile)]

        def compute(items, where, first=False):
            all_scores, all_values = [], []
            for i in items:
                slot, tile = i // TILES, i % TILES
                if i < MAIN:
                    query, episode = q_all[i], tile_episode(slot, tile)
                else:
                    query, episode = q_all[extra_tile[i - MAIN]], i - MAIN + 1
                parts, values = [], []
                for b in where:
                    if b == "new":
                        if prefill:
                            limit = row_block(slot) * ROWS + tile * TILE + lane_position
                        else:
                            limit = jnp.where(episode == 0, 2 * STRETCH, -1)
                        s = scores(fresh_all[:, :, :, 0:DIM].reshape(RING * 2 * NEW, DIM), query)
                        kept = []
                        for part in range(2 * RING):
                            base = part % 2 * STRETCH + blocks[part // 2] * NEW
                            kept.append(jnp.where(new_row <= limit - base, s[part * NEW:(part + 1) * NEW], MASKED))
                        parts.append(jnp.concatenate(kept, axis=0))
                        values.append(fresh_all[:, :, :, DIM:2 * DIM].reshape(RING * 2 * NEW, DIM))
                    else:
                        allowed = slot_row < len_ref[episode] - blocks[b] * SLOTS
                        parts.append(jnp.where(allowed, scores(buffers[b][episode, :, 0:DIM], query), MASKED))
                        values.append(buffers[b][episode, :, DIM:2 * DIM])
                all_scores.append(parts)
                all_values.append(values)
            update(items, all_scores, all_values, first)

        def state(slot, tile):
            i = slot * TILES + tile
            top, total, summed = acc_s[i, 0:1], acc_s[i, 1:2], acc_o[i]
            if prefill:
                return top, total, summed
            first = tile_episode(slot, tile)
            row_episode = jnp.zeros((1, LANES), jnp.int32)
            for r in range(TILE // STEPS):
                row_episode = jnp.where(
                    lane_position // STEPS == r, episode_ref[decode_row(slot, tile) + r], row_episode
                )
            for j in range(EXTRA):
                other = (row_episode == j + 1) & (first != j + 1)
                top = jnp.where(other, acc_s[MAIN + j, 0:1], top)
                total = jnp.where(other, acc_s[MAIN + j, 1:2], total)
                summed = jnp.where(other, acc_o[MAIN + j], summed)
            return top, total, summed

        def result(number, slot, part, into_o, into_s, device):
            n = (slot - 1) * 2 + part
            return (
                remote(RESULT + 2 * number, tx_o.at[n], into_o, device),
                remote(RESULT + 2 * number + 1, tx_s.at[n], into_s, device),
            )

        results = [
            result(0, 3, 0, mid_o.at[0], mid_s.at[0], q_right),
            result(1, 3, 1, mid_o.at[1], mid_s.at[1], q_left),
            result(2, 2, 1, fin_o.at[0, 1], fin_s.at[0, 1], q_right),
            result(3, 1, 0, fin_o.at[1, 0], fin_s.at[1, 0], q_left),
            result(4, 2, 0, fin_o.at[0, 0], fin_s.at[0, 0], q_right),
            result(5, 1, 1, fin_o.at[1, 1], fin_s.at[1, 1], q_left),
        ]

        def pack(slot, part, incoming=None):
            n = (slot - 1) * 2 + part
            for t in range(2):
                now = state(slot, part * 2 + t)
                if incoming is not None:
                    now = merge(now, load(mid_o.at[incoming], mid_s.at[incoming], t))
                tx_s[n, 2 * t:2 * t + 1] = now[0]
                tx_s[n, 2 * t + 1:2 * t + 2] = now[1]
                tx_o[n, t] = now[2].astype(jnp.bfloat16)

        def ship(number):
            for copy in results[number]:
                copy.start()

        def arrive(number):
            for copy in results[number]:
                copy.wait_recv()

        tx_s[...] = jnp.zeros_like(tx_s)
        pair.start()
        for h in range(2):
            from_right[0, h].start()
            from_left[0, 1 - h].start()
        for copy in queries[:4]:
            copy.start()
        if not prefill:
            for j in range(EXTRA):
                extra_tile[j] = 0
            for slot in range(RING):
                for tile in range(TILES):
                    low = tile_episode(slot, tile)
                    high = episode_ref[decode_row(slot, tile) + TILE // STEPS - 1]
                    for j in range(EXTRA):
                        hit = (low < j + 1) & (high >= j + 1)
                        extra_tile[j] = jnp.where(hit, slot * TILES + tile, extra_tile[j])
        compute(span(0, 4), [0], True)
        pair.wait_recv()
        from_right["new"].start()
        from_left["new"].start()
        for h in range(2):
            for e in (1, 2, 3):
                from_right[e, h].start()
                if not prefill:
                    from_left[e, 1 - h].start()
        hand_on(queries[0], queries[4])
        hand_on(queries[1], queries[5])

        def pass_on(side, key, *onward):
            {"right": from_right, "left": from_left, "low": far_low, "high": far_high}[side][key].wait_recv()
            if (side, key) in relays:
                relays[side, key].start()
            for copy in onward:
                copy.start()

        pass_on("right", (0, 0), far_low[0])
        pass_on("left", (0, 1), far_high[0])
        pass_on("right", (0, 1))
        pass_on("left", (0, 0))
        pass_on("right", "new", far_low["new"])
        pass_on("left", "new", far_high["new"])
        queries[2].wait_recv()
        queries[3].wait_recv()
        compute(span(4, 12), [0], True)
        if prefill:
            compute(span(0, 4), [1, 2])
            queries[4].wait_recv()
            queries[5].wait_recv()
            compute(span(12, 16), [0], True)
            compute(span(4, 8), [1, 2])
            compute(span(8, 12), [1, 2])
            compute(span(12, 16), [1, 2])
            for e in (0, "new"):
                far_low[e].wait_recv()
                far_high[e].wait_recv()
            last = ["new", 3]
            compute(span(12, 16), last)
        else:
            pass_on("right", (1, 0), far_low[1])
            pass_on("left", (1, 1), far_high[1])
            queries[4].wait_recv()
            queries[5].wait_recv()
            for e in (0, "new"):
                pass_on("low", e)
                pass_on("high", e)
            compute(span(12, 19), [0], True)
            pass_on("right", (2, 0), far_low[2])
            pass_on("left", (2, 1), far_high[2])
            compute(span(0, 4), ["new"])
            compute(span(4, 8), ["new"])
            pass_on("right", (3, 0), far_low[3])
            pass_on("left", (3, 1), far_high[3])
            compute(span(8, 12), ["new"])
            compute(span(12, 16), ["new"])
            for e in late:
                from_right[e, 1].wait_recv()
            compute(span(0, 8), [1])
            compute(span(8, 19), [1])
            for e in late:
                from_left[e, 0].wait_recv()
            compute(span(0, 8), [2])
            compute(span(8, 19), [2])
            for e in late:
                far_low[e].wait_recv()
                far_high[e].wait_recv()
            last = [3]
            compute(span(12, 19), last)
        pack(3, 0)
        ship(0)
        pack(3, 1)
        ship(1)
        compute(span(4, 12), last)
        pack(2, 1)
        ship(2)
        pack(1, 0)
        ship(3)
        arrive(0)
        pack(2, 0, 0)
        ship(4)
        arrive(1)
        pack(1, 1, 1)
        ship(5)
        compute(span(0, 4), last)

        for number in (2, 3, 4, 5):
            arrive(number)
        for tile in range(TILES):
            now = state(0, tile)
            for side in range(2):
                now = merge(now, load(fin_o.at[side, tile // 2], fin_s.at[side, tile // 2], tile % 2))
            whole = (now[2] * (1.0 / now[1])).T.astype(jnp.bfloat16)
            for h in range(HEADS):
                out_ref[tile, :, h * DIM:(h + 1) * DIM] = whole[h * TILE:(h + 1) * TILE]

        sent = [pair] + queries + [c for both in results for c in both]
        for table in (from_right, from_left, far_low, far_high, relays):
            sent += list(table.values())
        for copy in sent:
            copy.wait_send()

    @pl.when(grp == 0)
    def _():
        program(True)

    @pl.when(grp == 1)
    def _():
        program(False)


def local(queries, history_cache, fresh_cache, hist_len, decode_episode):
    vmem = pl.BlockSpec(memory_space=pltpu.VMEM)
    bf16, f32 = jnp.bfloat16, jnp.float32
    block = pltpu.VMEM((EPISODES, SLOTS, 2 * DIM), bf16)
    out = pl.pallas_call(
        kernel,
        out_shape=jax.ShapeDtypeStruct((TILES, TILE, HEADS * DIM), bf16),
        in_specs=[pl.BlockSpec(memory_space=pl.ANY)] * 5,
        out_specs=vmem,
        scratch_shapes=[
            pltpu.SMEM((EPISODES,), jnp.int32),
            pltpu.SMEM((512,), jnp.int32),
            block,
            block,
            block,
            block,
            pltpu.VMEM((RING, 2, NEW, 2 * DIM), bf16),
            pltpu.VMEM((MAIN, TILE, HEADS * DIM), bf16),
            pltpu.VMEM((MAIN + EXTRA, DIM, LANES), f32),
            pltpu.VMEM((MAIN + EXTRA, 8, LANES), f32),
            pltpu.VMEM((6, 2, DIM, LANES), bf16),
            pltpu.VMEM((6, 8, LANES), f32),
            pltpu.VMEM((2, 2, DIM, LANES), bf16),
            pltpu.VMEM((2, 8, LANES), f32),
            pltpu.VMEM((2, 2, 2, DIM, LANES), bf16),
            pltpu.VMEM((2, 2, 8, LANES), f32),
            pltpu.SMEM((EXTRA,), jnp.int32),
            pltpu.SemaphoreType.DMA((COPIES,)),
            pltpu.SemaphoreType.DMA((COPIES,)),
            pltpu.SemaphoreType.DMA((5,)),
        ],
        compiler_params=pltpu.CompilerParams(
            collective_id=0, has_side_effects=True, vmem_limit_bytes=56 * 1024 * 1024
        ),
    )(
        queries.reshape(TILES, TILE, HEADS * DIM),
        history_cache.reshape(EPISODES, SLOTS, 2 * DIM),
        fresh_cache.reshape(NEW, 2 * DIM),
        hist_len,
        decode_episode,
    )
    return out.reshape(1, ROWS, HEADS * DIM)


def solution(mesh):
    placed = (
        P("grp", "ctx", "head"),
        P(None, "ctx", "head", None),
        P("grp", "ctx", "head", None),
        P(),
        P(),
    )
    return jax.shard_map(
        local, mesh=mesh, in_specs=placed, out_specs=P("grp", "ctx", "head"), check_vma=False
    )
```

time: 280 us -> 47.3 us (0.17)
  waiting for transfers between devices: 132 us -> 0 us
  other arithmetic: 49.5 us -> 0 us
  Pallas kernels: 0 us -> 45.5 us
  matrix products: 29.8 us -> 0 us
  local copies, waits for them, and re-layouts: 30.5 us -> 1.67 us
  loops' own time: 23.2 us -> 0 us
  between operations: 13.5 us -> 0.01 us
    all_gather x1 -> x0, waiting for transfers between devices: 128 us -> none  [local(): slot_piece = lax.all_gather(slot_pool, 'ctx', axis=0, tiled=True)]
    pallas_call x0 -> x1, Pallas kernels: none -> 45.5 us  [local(): pl.pallas_call(kernel, out_shape=jax.ShapeDtypeStruct((TILES, TILE, HEADS...]
    dot_general x32 -> x0, matrix products: 29.8 us -> none  [the longest x16 16.6 us: update_state(): jnp.einsum('qhgk,khd->qhgd', weights.astype(jnp.bfloat16), value_part, pr...]
    reduce_sum x33 -> x0, other arithmetic: 25.8 us -> none  [the longest x16 13 us: update_state(): total_new = total_old * rescale + jnp.sum(weights, axis=-1)]
    another operation x1 -> x0, loops' own time: 23.2 us -> none  [local(): lax.scan(one_shard, initial, (piece_blocks, shard_ids))]
    and x16 -> x0, other arithmetic: 20 us -> none  [allowed_mask(): return same_episode & inside]
    squeeze x16 -> x0, local copies, waits for them, and re-layouts: 17.8 us -> none  [local(): lax.scan(one_shard, initial, (piece_blocks, shard_ids))]
    dynamic_slice x16 -> x0, local copies, waits for them, and re-layouts: 10.5 us -> none  [local(): lax.scan(one_shard, initial, (piece_blocks, shard_ids))]
  transfers between devices with their start and end apart: 2 -> 0, of which waited for: 2 -> 0; matrix products, arithmetic and copies ran while one was open for 1% -> 0% of each run, Pallas kernels for 0% -> 0%
where the time goes in v1:
time: 47.3 us; the launch traced here: 47.2 us
  Pallas kernels  45.5 us (96%)
  local copies, waits for them, and re-layouts  1.67 us (4%)
    pallas_call x1, Pallas kernels, local(): pl.pallas_call(kernel, out_shape=jax.ShapeDtypeStruct((TILES, TILE, HEADS...  45.5 us
    unnamed x1, local copies, waits for them, and re-layouts  1.67 us

profile of v1, /device:TPU:48, one launch (start us, length us, event | category | flops | bytes accessed | tf_op | source)
XLA Modules:
  0.0 47.2 jit_solution(12053508788892470993)
XLA Ops:
  0.0 45.5 %shard_map.55 = bf16[4,32,1024]{2,1,0:T(8,128)(2,1)} custom-call(bf16[4,32,1024]{2,1,0:T(8,128)(2,1)} %bitcast.6, bf16[4,256,256]{2,1,0:T(8,128)(2,1)} %bitcast.5, bf16[64,256]{1,0:T(8,128)(2,1)} %bitcast.7, s32[4]{0:T(128)} %len_in.1, s32[512]{0:T(512)} %episode_in.1), custom_call_target="tpu_custom_call" | custom-call | tf_op jit(solution)/shard_map/pallas_call | solution.py:480
  45.5 1.7 %copy.7 = bf16[1,128,1024]{2,1,0:T(8,128)(2,1)} copy(bf16[1,128,1024]{2,1,0:T(8,128)(2,1)} %bitcast.4) | data formatting | bytes 524288

commit v2 on v1

--- a/solution.py
+++ b/solution.py
@@ -283,6 +283,16 @@
                             kept.append(jnp.where(new_row <= limit - base, s[part * NEW:(part + 1) * NEW], MASKED))
                         parts.append(jnp.concatenate(kept, axis=0))
                         values.append(fresh_all[:, :, :, DIM:2 * DIM].reshape(RING * 2 * NEW, DIM))
+                    elif isinstance(b, str):
+                        t = 0 if b == "new0" else 1
+                        limit = row_block(slot) * ROWS + tile * TILE + lane_position
+                        s = scores(fresh_all[:, t, :, 0:DIM].reshape(RING * NEW, DIM), query)
+                        kept = []
+                        for part in range(RING):
+                            base = t * STRETCH + blocks[part] * NEW
+                            kept.append(jnp.where(new_row <= limit - base, s[part * NEW:(part + 1) * NEW], MASKED))
+                        parts.append(jnp.concatenate(kept, axis=0))
+                        values.append(fresh_all[:, t, :, DIM:2 * DIM].reshape(RING * NEW, DIM))
                     else:
                         allowed = slot_row < len_ref[episode] - blocks[b] * SLOTS
                         parts.append(jnp.where(allowed, scores(buffers[b][episode, :, 0:DIM], query), MASKED))
@@ -364,13 +374,12 @@
         pair.wait_recv()
         from_right["new"].start()
         from_left["new"].start()
-        for h in range(2):
-            for e in (1, 2, 3):
+
+        def send(h, *episodes):
+            for e in episodes:
                 from_right[e, h].start()
                 if not prefill:
                     from_left[e, 1 - h].start()
-        hand_on(queries[0], queries[4])
-        hand_on(queries[1], queries[5])
 
         def pass_on(side, key, *onward):
             {"right": from_right, "left": from_left, "low": far_low, "high": far_high}[side][key].wait_recv()
@@ -379,53 +388,64 @@
             for copy in onward:
                 copy.start()
 
+        send(0, 1, 2, 3)
+        if prefill:
+            send(1, 1, 2, 3)
+        hand_on(queries[0], queries[4])
+        hand_on(queries[1], queries[5])
         pass_on("right", (0, 0), far_low[0])
         pass_on("left", (0, 1), far_high[0])
+        if not prefill:
+            send(1, 1)
         pass_on("right", (0, 1))
         pass_on("left", (0, 0))
         pass_on("right", "new", far_low["new"])
         pass_on("left", "new", far_high["new"])
+        if not prefill:
+            send(1, 2, 3)
         queries[2].wait_recv()
         queries[3].wait_recv()
         compute(span(4, 12), [0], True)
         if prefill:
             compute(span(0, 4), [1, 2])
+            compute(span(4, 8), [1, 2])
+            compute(span(8, 12), [1, 2])
             queries[4].wait_recv()
             queries[5].wait_recv()
-            compute(span(12, 16), [0], True)
-            compute(span(4, 8), [1, 2])
-            compute(span(8, 12), [1, 2])
-            compute(span(12, 16), [1, 2])
+            compute(span(12, 16), [0, 1, 2], True)
             for e in (0, "new"):
                 far_low[e].wait_recv()
                 far_high[e].wait_recv()
-            last = ["new", 3]
+            last = ["new0", 3]
+
+            def second(*slots):
+                for slot in slots:
+                    pl.when(row_block(slot) * ROWS >= STRETCH)(
+                        functools.partial(compute, span(slot * TILES, slot * TILES + TILES), ["new1"]))
+
             compute(span(12, 16), last)
+            second(3)
         else:
-            pass_on("right", (1, 0), far_low[1])
-            pass_on("left", (1, 1), far_high[1])
+            for e in late:
+                pass_on("right", (e, 0), far_low[e])
+                pass_on("left", (e, 1), far_high[e])
+            pass_on("low", 0)
+            pass_on("high", 0)
             queries[4].wait_recv()
             queries[5].wait_recv()
-            for e in (0, "new"):
-                pass_on("low", e)
-                pass_on("high", e)
             compute(span(12, 19), [0], True)
-            pass_on("right", (2, 0), far_low[2])
-            pass_on("left", (2, 1), far_high[2])
+            pass_on("low", "new")
+            pass_on("high", "new")
             compute(span(0, 4), ["new"])
-            compute(span(4, 8), ["new"])
-            pass_on("right", (3, 0), far_low[3])
-            pass_on("left", (3, 1), far_high[3])
-            compute(span(8, 12), ["new"])
-            compute(span(12, 16), ["new"])
+            for slot in range(1, RING):
+                compute(span(slot * TILES, slot * TILES + TILES), ["new"])
             for e in late:
                 from_right[e, 1].wait_recv()
-            compute(span(0, 8), [1])
-            compute(span(8, 19), [1])
-            for e in late:
                 from_left[e, 0].wait_recv()
-            compute(span(0, 8), [2])
-            compute(span(8, 19), [2])
+            compute(span(0, 5), [1, 2])
+            compute(span(5, 10), [1, 2])
+            compute(span(10, 15), [1, 2])
+            compute(span(15, 19), [1, 2])
             for e in late:
                 far_low[e].wait_recv()
                 far_high[e].wait_recv()
@@ -435,9 +455,17 @@
         ship(0)
         pack(3, 1)
         ship(1)
-        compute(span(4, 12), last)
-        pack(2, 1)
-        ship(2)
+        if prefill:
+            compute(span(8, 12), last)
+            second(2)
+            pack(2, 1)
+            ship(2)
+            compute(span(4, 8), last)
+            second(1)
+        else:
+            compute(span(4, 12), last)
+            pack(2, 1)
+            ship(2)
         pack(1, 0)
         ship(3)
         arrive(0)
@@ -447,6 +475,8 @@
         pack(1, 1, 1)
         ship(5)
         compute(span(0, 4), last)
+        if prefill:
+            second(0)
 
         for number in (2, 3, 4, 5):
             arrive(number)

time: 47.3 us -> 44.2 us (0.934)
  Pallas kernels: 45.5 us -> 42.4 us
    pallas_call x1, Pallas kernels: 45.5 us -> 42.4 us  [local(): pl.pallas_call(kernel, out_shape=jax.ShapeDtypeStruct((TILES, TILE, HEADS...]
where the time goes in v2:
time: 44.2 us; the launch traced here: 44 us
  Pallas kernels  42.4 us (96%)
  local copies, waits for them, and re-layouts  1.67 us (4%)
    pallas_call x1, Pallas kernels, local(): pl.pallas_call(kernel, out_shape=jax.ShapeDtypeStruct((TILES, TILE, HEADS...  42.4 us
    unnamed x1, local copies, waits for them, and re-layouts  1.67 us

profile of v2, /device:TPU:48, one launch (start us, length us, event | category | flops | bytes accessed | tf_op | source)
XLA Modules:
  0.0 44.0 jit_solution(4987801881843826322)
XLA Ops:
  0.0 42.4 %shard_map.55 = bf16[4,32,1024]{2,1,0:T(8,128)(2,1)} custom-call(bf16[4,32,1024]{2,1,0:T(8,128)(2,1)} %bitcast.6, bf16[4,256,256]{2,1,0:T(8,128)(2,1)} %bitcast.5, bf16[64,256]{1,0:T(8,128)(2,1)} %bitcast.7, s32[4]{0:T(128)} %len_in.1, s32[512]{0:T(512)} %episode_in.1), custom_call_target="tpu_custom_call" | custom-call | tf_op jit(solution)/shard_map/pallas_call | solution.py:510
  42.4 1.7 %copy.7 = bf16[1,128,1024]{2,1,0:T(8,128)(2,1)} copy(bf16[1,128,1024]{2,1,0:T(8,128)(2,1)} %bitcast.4) | data formatting | bytes 524288

commit v3 on v2

--- a/solution.py
+++ b/solution.py
@@ -58,6 +58,24 @@
             device_id=device, device_id_type=MESH,
         )
 
+    barrier = pltpu.get_barrier_semaphore()
+
+    def greet(device):
+        pl.semaphore_signal(barrier, inc=1, device_id=device, device_id_type=MESH)
+
+    greet(partner)
+    greet(x_right)
+    greet(x_left)
+
+    @pl.when(core == 0)
+    def _():
+        greet(direct)
+
+    @pl.when(core + grp > 0)
+    def _():
+        greet(z_right)
+        greet(z_left)
+
     local_copies = [
         pltpu.make_async_copy(src, dst, inside.at[n])
         for n, (src, dst) in enumerate([
@@ -68,27 +86,7 @@
     for copy in local_copies:
         copy.start()
 
-    barrier = pltpu.get_barrier_semaphore()
-
-    def greet(device):
-        pl.semaphore_signal(barrier, inc=1, device_id=device, device_id_type=MESH)
-
-    greet(partner)
-    greet(x_right)
-    greet(x_left)
-
-    @pl.when(core == 0)
-    def _():
-        greet(direct)
-
-    @pl.when(core + grp > 0)
-    def _():
-        greet(z_right)
-        greet(z_left)
-
     pl.semaphore_wait(barrier, jnp.where(core == 1, 5, 4 + 2 * grp))
-    for copy in local_copies:
-        copy.wait()
 
     lane = lax.broadcasted_iota(jnp.int32, (1, LANES), 1)
     lane_position = lane % TILE
@@ -353,13 +351,21 @@
             for copy in results[number]:
                 copy.wait_recv()
 
-        tx_s[...] = jnp.zeros_like(tx_s)
+        def settle():
+            for copy in local_copies:
+                copy.wait()
+            tx_s[...] = jnp.zeros_like(tx_s)
+
+        if prefill:
+            settle()
         pair.start()
         for h in range(2):
             from_right[0, h].start()
             from_left[0, 1 - h].start()
         for copy in queries[:4]:
             copy.start()
+        if not prefill:
+            settle()
         if not prefill:
             for j in range(EXTRA):
                 extra_tile[j] = 0
@@ -407,9 +413,7 @@
         queries[3].wait_recv()
         compute(span(4, 12), [0], True)
         if prefill:
-            compute(span(0, 4), [1, 2])
-            compute(span(4, 8), [1, 2])
-            compute(span(8, 12), [1, 2])
+            compute(span(0, 12), [1, 2])
             queries[4].wait_recv()
             queries[5].wait_recv()
             compute(span(12, 16), [0, 1, 2], True)
@@ -436,16 +440,13 @@
             compute(span(12, 19), [0], True)
             pass_on("low", "new")
             pass_on("high", "new")
-            compute(span(0, 4), ["new"])
-            for slot in range(1, RING):
-                compute(span(slot * TILES, slot * TILES + TILES), ["new"])
+            compute(span(0, 8), ["new"])
+            compute(span(8, 16), ["new"])
             for e in late:
                 from_right[e, 1].wait_recv()
                 from_left[e, 0].wait_recv()
-            compute(span(0, 5), [1, 2])
-            compute(span(5, 10), [1, 2])
-            compute(span(10, 15), [1, 2])
-            compute(span(15, 19), [1, 2])
+            compute(span(0, 10), [1, 2])
+            compute(span(10, 19), [1, 2])
             for e in late:
                 far_low[e].wait_recv()
                 far_high[e].wait_recv()

time: 44.2 us -> 45.6 us (1.032)
  the two profiles are of different devices: /device:TPU:48 before, /device:TPU:1 now
where the time goes in v3:
time: 45.6 us; the launch traced here: 45.5 us
  Pallas kernels  43.8 us (96%)
  local copies, waits for them, and re-layouts  1.67 us (4%)
    pallas_call x1, Pallas kernels, local(): pl.pallas_call(kernel, out_shape=jax.ShapeDtypeStruct((TILES, TILE, HEADS...  43.8 us
    unnamed x1, local copies, waits for them, and re-layouts  1.67 us

profile of v3, /device:TPU:1, one launch (start us, length us, event | category | flops | bytes accessed | tf_op | source)
XLA Modules:
  0.0 45.5 jit_solution(17909191491510142375)
XLA Ops:
  0.0 43.8 %shard_map.55 = bf16[4,32,1024]{2,1,0:T(8,128)(2,1)} custom-call(bf16[4,32,1024]{2,1,0:T(8,128)(2,1)} %bitcast.6, bf16[4,256,256]{2,1,0:T(8,128)(2,1)} %bitcast.5, bf16[64,256]{1,0:T(8,128)(2,1)} %bitcast.7, s32[4]{0:T(128)} %len_in.1, s32[512]{0:T(512)} %episode_in.1), custom_call_target="tpu_custom_call" | custom-call | tf_op jit(solution)/shard_map/pallas_call | solution.py:511
  43.8 1.7 %copy.7 = bf16[1,128,1024]{2,1,0:T(8,128)(2,1)} copy(bf16[1,128,1024]{2,1,0:T(8,128)(2,1)} %bitcast.4) | data formatting | bytes 524288
